TPU v7x, 1024 devices: a whole 8x8x8 slice. The times are simulated.
1024 devices in a mesh: section: 16 (over y, core), dp: 64 (over x, z).
Axes of the slice: x: 8, y: 8, z: 8, core: 2. Of those that a mesh axis runs over, the one named last changes fastest.
Arguments:
- emb_rows: bfloat16 [65536, 7168], P('dp', 'section'), may hold values from -6 to 6
- grad_normed: bfloat16 [65536, 7168], P('dp', 'section'), may hold values from -6 to 6
- norm_gain: float32 [7168], P('section'), may hold values from 0.25 to 1.75
- owner_shard: int32 [65536, 1], P('dp'), may hold values from 0 to 63; in each aligned block of 1024 rows (0 to 1023, 1024 to 2047, ...) at most 24 rows name the same one
- row_in_shard: int32 [65536, 1], P('dp'), may hold values from 0 to 2019
Outputs:
- table_grad: bfloat16 [129280, 7168], P('dp', 'section')
- gain_gradient: float32 [7168], P('section')
Inputs may be any that keep to these rules, and one draw needn't show every extreme that they name: `owner_shard`: among the rows of one device, at most 24 name any one shard, a bound that some block reaches.
All inputs are finite; a program needn't handle non-finite values.
Results may differ from a plain program's by a relative error of at most 0.0045.
Values may be sent and summed in bfloat16 or wider, within the bound.
No kernel may reach another device: no remote copies, remote signals or barrier semaphores. Data moves between devices by JAX's collectives and lax.ppermute only.
A program may use at most 32 MiB of HBM per device.

v0:
```python
import math

import jax
import jax.numpy as jnp
from jax import lax
from jax.sharding import PartitionSpec as P

MODEL_WIDTH = 7168
VOCAB = 129280


EPS = 1e-06


def table_sum(ids, rows, vocab_dev):
    slots = ids.shape[0]
    block = math.gcd(slots, 256)
    ids_b = ids.reshape(slots // block, block)
    rows_b = rows.reshape(slots // block, block, rows.shape[1])
    vocab_rows = jnp.arange(vocab_dev, dtype=jnp.int32)

    def step(total, pair):
        id_block, row_block = pair
        onehot = (vocab_rows[:, None] == id_block[None, :]).astype(jnp.bfloat16)
        return (total + jnp.dot(onehot, row_block, preferred_element_type=jnp.float32), None)

    start = jnp.zeros((vocab_dev, rows.shape[1]), jnp.float32)
    total, _ = lax.scan(step, start, (ids_b, rows_b))
    return total


def on_device(emb_rows, grad_normed, norm_gain, owner_shard, row_in_shard):
    tok_rows = emb_rows.shape[0]
    columns = emb_rows.shape[1]
    shards = lax.axis_size("dp")
    capacity = max(2, 3 * tok_rows // (2 * shards))
    vocab_dev = VOCAB // shards
    embedding_rows = emb_rows.astype(jnp.float32)
    output_gradient = grad_normed.astype(jnp.float32)
    gained_gradient = norm_gain[None, :] * output_gradient
    sq = lax.psum(jnp.sum(embedding_rows * embedding_rows, axis=1), "section")
    inverse_norm = lax.rsqrt(sq / MODEL_WIDTH + EPS)
    normalized_rows = embedding_rows * inverse_norm[:, None]
    scaled_rows = lax.psum(jnp.sum(gained_gradient * normalized_rows, axis=1), "section")
    embedding_gradient = (
        (gained_gradient - normalized_rows * (scaled_rows / MODEL_WIDTH)[:, None])
        * inverse_norm[:, None]
    ).astype(jnp.bfloat16)
    gain_gradient = lax.psum(jnp.sum(output_gradient * normalized_rows, axis=0), "dp")
    targets = owner_shard[:, 0]
    marks = (targets[:, None] == jnp.arange(shards, dtype=jnp.int32)[None, :]).astype(jnp.int32)
    before = jnp.cumsum(marks, axis=0) - marks
    position = targets * capacity + jnp.sum(before * marks, axis=1)
    row_buffer = (
        jnp.zeros((shards * capacity, columns), jnp.bfloat16).at[position].set(embedding_gradient)
    )
    row_buffer = row_buffer.reshape(shards, capacity, columns)
    id_buffer = jnp.full((shards * capacity,), -1, jnp.int32).at[position].set(row_in_shard[:, 0])
    id_buffer = id_buffer.reshape(shards, capacity)
    got_rows, got_ids = (
        lax.all_to_all(row_buffer, "dp", split_axis=0, concat_axis=0, tiled=True),
        lax.all_to_all(id_buffer, "dp", split_axis=0, concat_axis=0, tiled=True),
    )
    table = table_sum(got_ids.reshape(-1), got_rows.reshape(-1, columns), vocab_dev)
    return (table.astype(jnp.bfloat16), gain_gradient)


def solution(mesh):
    return jax.shard_map(
        on_device,
        mesh=mesh,
        in_specs=(
            P("dp", "section"),
            P("dp", "section"),
            P("section"),
            P("dp", None),
            P("dp", None),
        ),
        out_specs=(P("dp", "section"), P("section")),
        check_vma=False,
    )
```

profile of v0, /device:TPU:8, one launch (start us, length us, event | category | flops | bytes accessed | tf_op | source)
XLA Modules:
  0.0 319.4 jit_solution(1255331029858492943)
XLA Ops:
  0.6 0.0 copy-start.2
  0.6 0.0 copy-start
  0.7 0.0 copy-start.1
  0.7 0.0 copy-start.3
  0.7 0.8 fusion.20
  1.5 18.0 %reduce-window.6 = s32[64,8,128]{2,1,0:T(8,128)S(1)} reduce-window(s32[64,8,128]{2,1,0:T(8,128)S(1)} %fusion.20, s32[]{:T(128)} %constant.8.clone.1), window={size=1x1x128 pad=0_0x0_0x127_0}, to_apply=%region_0.0 | reduce-window | flops 8323072 | bytes 524292 | tf_op jit(solution)/shard_map/reduce-window
  19.5 0.1 slice.8
  19.7 0.1 copy.10
  19.8 0.1 copy.11
  19.9 0.1 broadcast_add_fusion
  20.1 0.0 copy-done.2
  20.1 0.1 fusion.19
  20.2 4.5 %scatter_custom_fusion = s32[1536]{0:T(1024)S(1)} fusion(s32[1024]{0:T(1024)S(1)} %bitcast.41, s32[1024]{0:T(1024)} %bitcast.43, s32[]{:T(128)} %constant.9.clone.1), kind=kCustom, calls=%fused_computation.34 | custom fusion | bytes 6656 | tf_op jit(solution)/shard_map/scatter | solution.py:58
  24.7 0.7 all_to_all.9
  25.3 22.7 %all-to-all-start = ((s32[64,1,24]{2,1,0:T(1,128)}), s32[64,1,24]{2,1,0:T(1,128)S(1)}, u32[]{:S(2)}, u32[]{:S(2)}) async-start(s32[64,1,24]{2,1,0:T(1,128)} %bitcast.7), calls=%async_computation | async-start | bytes 65536 | tf_op jit(solution)/shard_map/all_to_all | solution.py:62
  48.1 0.0 copy-done
  48.1 0.2 fusion.14
  48.3 27.0 %psum.21 = f32[1024]{0:T(1024)S(1)} all-reduce(f32[1024]{0:T(1024)S(1)} %fusion.14), channel_id=1, replica_groups=mesh['section'=16,'dp'=64] {'section'}, use_global_device_ids=true, to_apply=%region_5.0 | all-reduce | flops 1024 | bytes 8192 | tf_op jit(solution)/shard_map/psum | solution.py:41
  75.3 0.0 copy-done.1
  75.3 0.0 copy-done.3
  75.3 0.7 fusion.13
  76.0 23.5 %psum.22 = f32[1024]{0:T(1024)S(1)} all-reduce(f32[1024]{0:T(1024)S(1)} %get-tuple-element.48), channel_id=1, replica_groups=mesh['section'=16,'dp'=64] {'section'}, use_global_device_ids=true, to_apply=%region_7.8 | all-reduce | flops 1024 | bytes 8192 | tf_op jit(solution)/shard_map/psum | solution.py:44
  99.5 0.5 fusion.11
  100.0 0.5 copy.13
  100.5 6.4 %scatter_custom_fusion.1 = bf16[1536,448]{1,0:T(8,128)(2,1)} fusion(s32[1024]{0:T(1024)S(1)} %bitcast.42, bf16[1024,448]{1,0:T(8,128)(2,1)S(1)} %copy.13, bf16[]{:T(256)} %constant.30.clone.1), kind=kCustom, calls=%fused_computation.22 | custom fusion | bytes 1376258 | tf_op jit(solution)/shard_map/scatter | solution.py:55
  106.9 0.0 all-to-all-done
  106.9 12.4 %all-to-all-start.1 = ((bf16[64,24,448]{2,1,0:T(8,128)(2,1)}), bf16[64,24,448]{2,1,0:T(8,128)(2,1)S(1)}, u32[]{:S(2)}, u32[]{:S(2)}) async-start(bf16[64,24,448]{2,1,0:T(8,128)(2,1)} %bitcast.8), calls=%async_computation.1 | async-start | bytes 3145728 | tf_op jit(solution)/shard_map/all_to_all | solution.py:61
  119.3 169.2 %psum.23 = f32[448]{0:T(512)} all-reduce(f32[448]{0:T(512)S(1)} %get-tuple-element.47), channel_id=1, replica_groups=mesh['section'=16,'dp'=64] {'dp'}, use_global_device_ids=true, to_apply=%region_12.13 | all-reduce | flops 448 | bytes 3584 | tf_op jit(solution)/shard_map/psum | solution.py:49
  288.5 0.6 broadcast.52
  289.1 0.8 reduce.3
  289.9 0.1 reshape_reshape.6
  290.0 0.0 all-to-all-done.1
  290.0 25.8 %while.11 = (s32[]{:T(128)}, f32[2020,448]{0,1:T(8,128)}, s32[6,256]{1,0:T(8,128)S(1)}, bf16[6,256,448]{2,1,0:T(8,128)(2,1)S(1)}, s32[]{:T(128)}, /*index=5*/s32[]{:T(128)}) while((s32[]{:T(128)}, f32[2020,448]{0,1:T(8,128)}, s32[6,256]{1,0:T(8,128)S(1)}, bf16[6,256,448]{2,1,0:T(8,128)(2,1)S(1)}, s32[]{:T(128)}, ...), condition=%wide.region_10.11_spmd.clone, body=%wide.region_9.10_spmd.clone.sunk | while | flops 465666560 | bytes 7504983 | solution.py:28
  290.0 2.6 select_add_fusion.2
  292.6 4.6 %select_add_fusion.2 = f32[2020,448]{0,1:T(8,128)} fusion(f32[2020,448]{0,1:T(8,128)} %get-tuple-element.89, pred[]{:T(512)S(6)} %compare.3, s32[256]{0:T(256)S(1)} %bitcast.36, bf16[6,256,448]{2,1,0:T(8,128)(2,1)S(1)} %get-tuple-element.97, s32[]{:T(128)} %get-tuple-element.88), kind=kOutput, calls=%fused_computation.3.clone.1 | convolution fusion | flops 465666560 | bytes 7502853 | tf_op jit(solution)/shard_map/while/body/eval_jaxpr/dot_general | solution.py:25
  297.3 4.6 %select_add_fusion.2 = f32[2020,448]{0,1:T(8,128)} fusion(f32[2020,448]{0,1:T(8,128)} %get-tuple-element.89, pred[]{:T(512)S(6)} %compare.3, s32[256]{0:T(256)S(1)} %bitcast.36, bf16[6,256,448]{2,1,0:T(8,128)(2,1)S(1)} %get-tuple-element.97, s32[]{:T(128)} %get-tuple-element.88), kind=kOutput, calls=%fused_computation.3.clone.1 | convolution fusion | flops 465666560 | bytes 7502853 | tf_op jit(solution)/shard_map/while/body/eval_jaxpr/dot_general | solution.py:25
  301.9 4.6 %select_add_fusion.2 = f32[2020,448]{0,1:T(8,128)} fusion(f32[2020,448]{0,1:T(8,128)} %get-tuple-element.89, pred[]{:T(512)S(6)} %compare.3, s32[256]{0:T(256)S(1)} %bitcast.36, bf16[6,256,448]{2,1,0:T(8,128)(2,1)S(1)} %get-tuple-element.97, s32[]{:T(128)} %get-tuple-element.88), kind=kOutput, calls=%fused_computation.3.clone.1 | convolution fusion | flops 465666560 | bytes 7502853 | tf_op jit(solution)/shard_map/while/body/eval_jaxpr/dot_general | solution.py:25
  306.5 4.6 %select_add_fusion.2 = f32[2020,448]{0,1:T(8,128)} fusion(f32[2020,448]{0,1:T(8,128)} %get-tuple-element.89, pred[]{:T(512)S(6)} %compare.3, s32[256]{0:T(256)S(1)} %bitcast.36, bf16[6,256,448]{2,1,0:T(8,128)(2,1)S(1)} %get-tuple-element.97, s32[]{:T(128)} %get-tuple-element.88), kind=kOutput, calls=%fused_computation.3.clone.1 | convolution fusion | flops 465666560 | bytes 7502853 | tf_op jit(solution)/shard_map/while/body/eval_jaxpr/dot_general | solution.py:25
  311.2 4.6 %select_add_fusion.2 = f32[2020,448]{0,1:T(8,128)} fusion(f32[2020,448]{0,1:T(8,128)} %get-tuple-element.89, pred[]{:T(512)S(6)} %compare.3, s32[256]{0:T(256)S(1)} %bitcast.36, bf16[6,256,448]{2,1,0:T(8,128)(2,1)S(1)} %get-tuple-element.97, s32[]{:T(128)} %get-tuple-element.88), kind=kOutput, calls=%fused_computation.3.clone.1 | convolution fusion | flops 465666560 | bytes 7502853 | tf_op jit(solution)/shard_map/while/body/eval_jaxpr/dot_general | solution.py:25
  315.8 3.5 %convert_element_type.25 = bf16[2020,448]{0,1:T(8,128)(2,1)} convert(f32[2020,448]{0,1:T(8,128)} %get-tuple-element.29) | non-fusion elementwise | flops 904960 | bytes 5429760 | tf_op jit(solution)/shard_map/convert_element_type | solution.py:65
  (12 shorter events, 0.1 us)
Async XLA Ops:
  0.6 19.4 %copy-start.2 = (s32[1024,1]{0,1:T(1,128)S(1)}, s32[1024,1]{0,1:T(1,128)}, u32[]{:S(2)}) copy-start(s32[1024,1]{0,1:T(1,128)} %param.10) | copy-start | bytes 12292
  0.6 47.4 %copy-start = (bf16[1024,448]{0,1:T(8,128)(2,1)S(1)}, bf16[1024,448]{0,1:T(8,128)(2,1)}, u32[]{:S(2)}) copy-start(bf16[1024,448]{0,1:T(8,128)(2,1)} %param.7) | copy-start | bytes 2752516
  0.7 74.6 %copy-start.1 = (bf16[1024,448]{0,1:T(8,128)(2,1)S(1)}, bf16[1024,448]{0,1:T(8,128)(2,1)}, u32[]{:S(2)}) copy-start(bf16[1024,448]{0,1:T(8,128)(2,1)} %param.8) | copy-start | bytes 2752516
  0.7 74.6 %copy-start.3 = (f32[448]{0:T(512)S(1)}, f32[448]{0:T(512)}, u32[]{:S(2)}) copy-start(f32[448]{0:T(512)} %param.9) | copy-start | bytes 5380
  25.3 81.6 %all-to-all-start = ((s32[64,1,24]{2,1,0:T(1,128)}), s32[64,1,24]{2,1,0:T(1,128)S(1)}, u32[]{:S(2)}, u32[]{:S(2)}) async-start(s32[64,1,24]{2,1,0:T(1,128)} %bitcast.7), calls=%async_computation | async-start | bytes 65536 | tf_op jit(solution)/shard_map/all_to_all | solution.py:62
  106.9 183.0 %all-to-all-start.1 = ((bf16[64,24,448]{2,1,0:T(8,128)(2,1)}), bf16[64,24,448]{2,1,0:T(8,128)(2,1)S(1)}, u32[]{:S(2)}, u32[]{:S(2)}) async-start(bf16[64,24,448]{2,1,0:T(8,128)(2,1)} %bitcast.8), calls=%async_computation.1 | async-start | bytes 3145728 | tf_op jit(solution)/shard_map/all_to_all | solution.py:61
where the time goes:
time: 320 us; the launch traced here: 319 us
  blocking collectives  220 us (69%)
  starting transfers between devices  35.1 us (11%)
  matrix products  25.8 us (8%)
  other arithmetic  24.8 us (8%)
  local copies, waits for them, and re-layouts  13.1 us (4%)
    psum x1, blocking collectives, on_device(): lax.psum(jnp.sum(output_gradient * normalized_rows, axis=0), 'dp')  169 us
    psum x1, blocking collectives, on_device(): sq = lax.psum(jnp.sum(embedding_rows * embedding_rows, axis=1), 'section')  27 us
    dot_general x6, matrix products, step(): jnp.dot(onehot, row_block, preferred_element_type=jnp.float32)  25.8 us
    psum x1, blocking collectives, on_device(): lax.psum(jnp.sum(gained_gradient * normalized_rows, axis=1), 'section')  23.5 us
    all_to_all x1, starting transfers between devices, on_device(): lax.all_to_all(id_buffer, 'dp', split_axis=0, concat_axis=0, tiled=True)  22.7 us
    another operation x3, other arithmetic  18.2 us
    all_to_all x1, starting transfers between devices, on_device(): lax.all_to_all(row_buffer, 'dp', split_axis=0, concat_axis=0, tiled=True)  12.4 us
  transfers between devices with their start and end apart: 2, of which 0 were waited for; matrix products, arithmetic and copies ran while one was open for 3% of the time, Pallas kernels for 0%

commit v1 on v0

v1 whole, which is shorter than its diff:
```python
import jax
import jax.numpy as jnp
from jax import lax
from jax.experimental import pallas as pl
from jax.experimental.pallas import tpu as pltpu
from jax.sharding import PartitionSpec as P

MODEL_WIDTH = 7168
VOCAB = 129280
EPS = 1e-06
LANES = 128
STRIP = 16
PIECES = 3
GAP = 8
VMEM_LIMIT = 40 * 1024 * 1024


def iota(shape, dim):
    return lax.broadcasted_iota(jnp.int32, shape, dim)


def column_of(row):
    n = row.shape[1]
    return jnp.sum(jnp.where(iota((n, n), 0) == iota((n, n), 1), row, 0.0), axis=1, keepdims=True)


def fold_mask(n, width, first, lane_dim):
    shape = (n, LANES) if lane_dim == 1 else (LANES, n)
    lane = iota(shape, lane_dim) - first
    feature = iota(shape, 1 - lane_dim)
    hit = feature == lane
    for r in range(1, n // width):
        hit = hit | (feature - r * width == lane)
    return hit & (lane >= 0) & (lane < width)


def row_mask(n, width):
    offset = iota((8, n), 1) - iota((8, n), 0) * width
    return (offset >= 0) & (offset < width)


def stats_kernel(e_ref, dy_ref, gain_ref, out_ref):
    width, tokens = e_ref.shape
    gain = column_of(gain_ref[...])
    sq = jnp.zeros((8, tokens), jnp.float32)
    dot = jnp.zeros((8, tokens), jnp.float32)
    for k in range(0, width, STRIP):
        e = e_ref[k : k + STRIP, :].astype(jnp.float32)
        dy = dy_ref[k : k + STRIP, :].astype(jnp.float32)
        ee = e * e
        ed = e * (dy * gain[k : k + STRIP])
        sq = sq + ee[:8] + ee[8:]
        dot = dot + ed[:8] + ed[8:]
    sub = iota((8, LANES), 0)
    halves = []
    for total in (sq, dot):
        total = jnp.sum(total, axis=0, keepdims=True)
        tile = jnp.zeros((8, LANES), jnp.float32)
        for s in range(tokens // LANES):
            tile = jnp.where(sub == s, total[:, s * LANES : (s + 1) * LANES], tile)
        halves.append(tile)
    pair = jnp.concatenate(halves, axis=1)
    out_ref[...] = jnp.broadcast_to(pair[None], out_ref.shape)


def position_of(owner, shards, capacity):
    tokens = owner.shape[1]
    blocks = tokens // LANES
    marks = (iota((shards, tokens), 0) == owner).astype(jnp.float32)
    stacked = jnp.concatenate([marks[:, b * LANES : (b + 1) * LANES] for b in range(blocks)], axis=0)
    earlier = (iota((LANES, LANES), 0) < iota((LANES, LANES), 1)).astype(jnp.bfloat16)
    before = jnp.dot(stacked.astype(jnp.bfloat16), earlier, preferred_element_type=jnp.float32)
    totals = jnp.sum(stacked, axis=1, keepdims=True)
    start = jnp.zeros((shards, 1), jnp.float32)
    ranks = []
    for b in range(blocks):
        rows = slice(b * shards, (b + 1) * shards)
        ranks.append(jnp.sum(stacked[rows] * (before[rows] + start), axis=0, keepdims=True))
        start = start + totals[rows]
    rank = jnp.concatenate(ranks, axis=1)
    return owner * capacity + rank.astype(jnp.int32)


def rows_kernel(shards, capacity, e_ref, dy_ref, gain_ref, stats_ref, owner_ref, row_ref, out_ref, rows_ref, part_ref):
    width, tokens = e_ref.shape
    padded = out_ref.shape[1]
    gain = column_of(gain_ref[...])
    pair = jnp.sum(stats_ref[...], axis=0)
    sq = jnp.concatenate([pair[s : s + 1, :LANES] for s in range(8)], axis=1)
    dot = jnp.concatenate([pair[s : s + 1, LANES:] for s in range(8)], axis=1)
    rinv = lax.rsqrt(sq / MODEL_WIDTH + EPS)
    pull = dot * rinv * rinv / MODEL_WIDTH
    for k in range(0, width, STRIP):
        e = e_ref[k : k + STRIP, :].astype(jnp.float32)
        dy = dy_ref[k : k + STRIP, :].astype(jnp.float32)
        rows_ref[k : k + STRIP, :] = ((dy * gain[k : k + STRIP] - e * pull) * rinv).astype(jnp.bfloat16)
        term = dy * (e * rinv)
        part = term[:, :LANES]
        for s in range(1, tokens // LANES):
            part = part + term[:, s * LANES : (s + 1) * LANES]
        part_ref[k : k + STRIP, :] = part
    ids = row_ref[...]
    sub = iota((padded - width, tokens), 0)
    rows_ref[width:, :] = jnp.where(
        sub == 0, ids >> 3, jnp.where(sub == 1, ids & 7, 0)
    ).astype(jnp.float32).astype(jnp.bfloat16)
    span = padded - width - GAP
    first = LANES - span
    partial = jnp.sum(part_ref[...], axis=1, keepdims=True)
    spread = jnp.where(fold_mask(width, span, first, 1), partial, 0.0)
    fold = jnp.dot(
        row_mask(width, span).astype(jnp.float32), spread,
        precision=lax.Precision.HIGHEST, preferred_element_type=jnp.float32,
    )
    pieces = []
    for _ in range(PIECES):
        piece = fold.astype(jnp.bfloat16).astype(jnp.float32)
        pieces.append(piece)
        fold = fold - piece
    extra = jnp.concatenate(pieces, axis=0)
    position = position_of(owner_ref[...], shards, capacity)
    group = 8
    chunk = group * capacity
    rows = rows_ref[...]

    def step(i, carry):
        slot = iota((chunk, tokens), 0) + i * chunk
        pick = (slot == position).astype(jnp.float32).astype(jnp.bfloat16)
        got = lax.dot_general(pick, rows, (((1,), (1,)), ((), ())), preferred_element_type=jnp.float32)
        last = got[:, padded - LANES :].reshape(group, capacity, LANES) + extra[None]
        where = pl.ds(pl.multiple_of(i * chunk, chunk), chunk)
        out_ref[where, : padded - LANES] = got[:, : padded - LANES].astype(jnp.bfloat16)
        out_ref[where, padded - LANES :] = last.reshape(chunk, LANES).astype(jnp.bfloat16)
        return carry

    lax.fori_loop(0, shards // group, step, 0)


def table_kernel(capacity, width, got_ref, table_ref, gain_ref, turned_ref, id_ref):
    slots, padded = got_ref.shape
    tile = table_ref.shape[1]
    j = pl.program_id(0)

    @pl.when(j == 0)
    def _():
        turned_ref[...] = got_ref[...].T
        last = got_ref[:, padded - LANES :].astype(jnp.float32)
        lane = width - (padded - LANES)
        id_ref[...] = (last[:, lane : lane + 1] * 8.0 + last[:, lane + 1 : lane + 2]).astype(jnp.int32)
        total = jnp.sum(last.reshape(slots // capacity, capacity, LANES), axis=0)
        fold = total[:8] + total[8:16] + total[16:24]
        span = padded - width - GAP
        spread = jnp.dot(
            fold, fold_mask(width, span, LANES - span, 0).astype(jnp.float32),
            precision=lax.Precision.HIGHEST, preferred_element_type=jnp.float32,
        )
        gain_ref[...] = jnp.sum(jnp.where(row_mask(width, span), spread, 0.0), axis=0, keepdims=True)

    vocab = iota((slots, tile), 1) + j * tile
    onehot = (vocab == id_ref[...]).astype(jnp.float32).astype(jnp.bfloat16)
    table_ref[...] = jnp.dot(
        turned_ref[:width, :], onehot, preferred_element_type=jnp.float32
    ).astype(jnp.bfloat16)


def on_device(emb_rows, grad_normed, norm_gain, owner_shard, row_in_shard):
    tokens, width = emb_rows.shape
    sections, shards = lax.axis_size("section"), lax.axis_size("dp")
    capacity = 3 * tokens // (2 * shards)
    vocab_dev = VOCAB // shards
    padded = -(-width // LANES) * LANES
    slots = shards * capacity
    e, dy = emb_rows.T, grad_normed.T
    gain = norm_gain.reshape(1, width)
    owner, row = owner_shard.reshape(1, tokens), row_in_shard.reshape(1, tokens)
    params = pltpu.CompilerParams(vmem_limit_bytes=VMEM_LIMIT)
    stats = pl.pallas_call(
        stats_kernel,
        out_shape=jax.ShapeDtypeStruct((sections, 8, 2 * LANES), jnp.float32),
        compiler_params=params,
    )(e, dy, gain)
    stats = lax.all_to_all(stats, "section", 0, 0, tiled=True)
    message = pl.pallas_call(
        lambda *refs: rows_kernel(shards, capacity, *refs),
        out_shape=jax.ShapeDtypeStruct((slots, padded), jnp.bfloat16),
        scratch_shapes=[pltpu.VMEM((padded, tokens), jnp.bfloat16), pltpu.VMEM((width, LANES), jnp.float32)],
        compiler_params=params,
    )(e, dy, gain, stats, owner, row)
    got = lax.all_to_all(message.reshape(shards, capacity, padded), "dp", 0, 0, tiled=True)
    tile = 512
    table, gain_gradient = pl.pallas_call(
        lambda *refs: table_kernel(capacity, width, *refs),
        grid=(pl.cdiv(vocab_dev, tile),),
        in_specs=[pl.BlockSpec((slots, padded), lambda j: (0, 0))],
        out_specs=[pl.BlockSpec((width, tile), lambda j: (0, j)), pl.BlockSpec((1, width), lambda j: (0, 0))],
        out_shape=[
            jax.ShapeDtypeStruct((width, vocab_dev), jnp.bfloat16),
            jax.ShapeDtypeStruct((1, width), jnp.float32),
        ],
        scratch_shapes=[pltpu.VMEM((padded, slots), jnp.bfloat16), pltpu.VMEM((slots, 1), jnp.int32)],
        compiler_params=params,
    )(got.reshape(slots, padded))
    return (table.T, gain_gradient.reshape(width))


def solution(mesh):
    return jax.shard_map(
        on_device,
        mesh=mesh,
        in_specs=(
            P("dp", "section"),
            P("dp", "section"),
            P("section"),
            P("dp", None),
            P("dp", None),
        ),
        out_specs=(P("dp", "section"), P("section")),
        check_vma=False,
    )
```

time: 320 us -> 96.8 us (0.30)
  the two profiles are of different devices: /device:TPU:8 before, /device:TPU:6 now
where the time goes in v1:
time: 96.8 us; the launch traced here: 96.5 us
  blocking collectives  82.5 us (85%)
  Pallas kernels  10.4 us (11%)
  local copies, waits for them, and re-layouts  3.05 us (3%)
    all_to_all x1, blocking collectives, on_device(): lax.all_to_all(message.reshape(shards, capacity, padded), 'dp', 0, 0, til...  66.3 us
    all_to_all x1, blocking collectives, on_device(): stats = lax.all_to_all(stats, 'section', 0, 0, tiled=True)  16.2 us
    pallas_call x1, Pallas kernels, on_device(): pl.pallas_call(lambda *refs: table_kernel(capacity, width, *refs), grid=(...  5.43 us
    pallas_call x1, Pallas kernels, on_device(): pl.pallas_call(lambda *refs: rows_kernel(shards, capacity, *refs), out_sh...  4.51 us
    unnamed x10, local copies, waits for them, and re-layouts  3.05 us

profile of v1, /device:TPU:6, one launch (start us, length us, event | category | flops | bytes accessed | tf_op | source)
XLA Modules:
  0.0 96.5 jit_solution(2227157817119864772)
XLA Ops:
  0.6 0.0 copy-start.3
  0.6 0.0 copy-start
  0.7 1.2 %copy-done = bf16[1024,448]{0,1:T(8,128)(2,1)S(1)} copy-done((bf16[1024,448]{0,1:T(8,128)(2,1)S(1)}, bf16[1024,448]{0,1:T(8,128)(2,1)}, u32[]{:S(2)}) %copy-start) | copy-done | bytes 917528
  1.8 0.0 copy-start.1
  1.8 1.2 %copy-done.1 = bf16[1024,448]{0,1:T(8,128)(2,1)S(1)} copy-done((bf16[1024,448]{0,1:T(8,128)(2,1)S(1)}, bf16[1024,448]{0,1:T(8,128)(2,1)}, u32[]{:S(2)}) %copy-start.1) | copy-done | bytes 917528
  3.0 0.0 copy-start.2
  3.0 0.7 copy-done.2
  3.7 0.0 copy-start.4
  3.7 0.4 shard_map.68
  4.1 16.2 %all_to_all.10.refs_3_ = f32[16,8,256]{2,1,0:T(8,128)S(1)} all-to-all(f32[16,8,256]{2,1,0:T(8,128)S(1)} %shard_map.68), channel_id=1, replica_groups=mesh['section'=16,'dp'=64] {'section'}, dimensions={0} | all-to-all | bytes 262144 | tf_op jit(solution)/shard_map/all_to_all | solution.py:182
  20.3 0.0 copy-done.3
  20.3 0.0 copy-done.4
  20.3 4.5 %shard_map.69 = bf16[1536,512]{1,0:T(8,128)(2,1)S(1)} custom-call(bf16[448,1024]{1,0:T(8,128)(2,1)S(1)} %bitcast.12, bf16[448,1024]{1,0:T(8,128)(2,1)S(1)} %bitcast.14, f32[1,448]{1,0:T(1,128)S(1)} %bitcast.16, f32[16,8,256]{2,1,0:T(8,128)S(1)} %all_to_all.10.refs_3_, s32[1,1024]{1,0:T(1,128)S(1)} %bitcast.17, s32[1,1024]{1,0:T(1,128)S(1)} %bitcast.18), custom_call_target="tpu_custom_call" | custom-call | tf_op jit(solution)/shard_map/pallas_call | solution.py:183
  24.8 66.3 %all_to_all.11 = bf16[64,24,512]{2,1,0:T(8,128)(2,1)S(1)} all-to-all(bf16[64,24,512]{2,1,0:T(8,128)(2,1)S(1)} %bitcast.10), channel_id=1, replica_groups=mesh['section'=16,'dp'=64] {'dp'}, dimensions={0} | all-to-all | bytes 3145728 | tf_op jit(solution)/shard_map/all_to_all | solution.py:189
  91.1 5.4 %shard_map.70 = (bf16[448,2020]{1,0:T(8,128)(2,1)}, f32[1,448]{1,0:T(1,128)}) custom-call(bf16[1536,512]{1,0:T(8,128)(2,1)S(1)} %bitcast.9), custom_call_target="tpu_custom_call" | custom-call | tf_op jit(solution)/shard_map/pallas_call | solution.py:191
Async XLA Ops:
  0.6 19.7 %copy-start.3 = (s32[1024,1]{0,1:T(1,128)S(1)}, s32[1024,1]{0,1:T(1,128)}, u32[]{:S(2)}) copy-start(s32[1024,1]{0,1:T(1,128)} %param.8) | copy-start | bytes 12292
  0.6 1.2 %copy-start = (bf16[1024,448]{0,1:T(8,128)(2,1)S(1)}, bf16[1024,448]{0,1:T(8,128)(2,1)}, u32[]{:S(2)}) copy-start(bf16[1024,448]{0,1:T(8,128)(2,1)} %param.5) | copy-start | bytes 2752516
  1.8 1.2 %copy-start.1 = (bf16[1024,448]{0,1:T(8,128)(2,1)S(1)}, bf16[1024,448]{0,1:T(8,128)(2,1)}, u32[]{:S(2)}) copy-start(bf16[1024,448]{0,1:T(8,128)(2,1)} %param.6) | copy-start | bytes 2752516
  3.0 0.7 copy-start.2
  3.7 16.6 %copy-start.4 = (s32[1024,1]{0,1:T(1,128)S(1)}, s32[1024,1]{0,1:T(1,128)}, u32[]{:S(2)}) copy-start(s32[1024,1]{0,1:T(1,128)} %param.9) | copy-start | bytes 12292

commit v2 on v1

--- a/solution.py
+++ b/solution.py
@@ -12,7 +12,11 @@
 STRIP = 16
 PIECES = 3
 GAP = 8
+LOADS = 2
 VMEM_LIMIT = 40 * 1024 * 1024
+FULL_VMEM = 62 * 1024 * 1024
+PICK = 16
+TILE = 1024
 
 
 def iota(shape, dim):
@@ -39,18 +43,40 @@
     return (offset >= 0) & (offset < width)
 
 
-def stats_kernel(e_ref, dy_ref, gain_ref, out_ref):
+def copies_of(pairs, sems, parts):
+    out = []
+    for p in range(parts):
+        group = []
+        for n, (source, target) in enumerate(pairs):
+            rows = source.shape[0] // parts
+            where = pl.ds(p * rows, rows)
+            group.append(pltpu.make_async_copy(source.at[where], target.at[where], sems.at[p, n]))
+        out.append(group)
+    return out
+
+
+def stats_kernel(e_hbm, dy_hbm, gain_hbm, out_ref, e_ref, dy_ref, gain_ref, sems, gain_sem):
     width, tokens = e_ref.shape
+    gain_copy = pltpu.make_async_copy(gain_hbm, gain_ref, gain_sem)
+    gain_copy.start()
+    copies = copies_of([(e_hbm, e_ref), (dy_hbm, dy_ref)], sems, LOADS)
+    for group in copies:
+        for copy in group:
+            copy.start()
+    gain_copy.wait()
     gain = column_of(gain_ref[...])
     sq = jnp.zeros((8, tokens), jnp.float32)
     dot = jnp.zeros((8, tokens), jnp.float32)
-    for k in range(0, width, STRIP):
-        e = e_ref[k : k + STRIP, :].astype(jnp.float32)
-        dy = dy_ref[k : k + STRIP, :].astype(jnp.float32)
-        ee = e * e
-        ed = e * (dy * gain[k : k + STRIP])
-        sq = sq + ee[:8] + ee[8:]
-        dot = dot + ed[:8] + ed[8:]
+    for p, group in enumerate(copies):
+        for copy in group:
+            copy.wait()
+        for k in range(p * width // LOADS, (p + 1) * width // LOADS, STRIP):
+            e = e_ref[k : k + STRIP, :].astype(jnp.float32)
+            dy = dy_ref[k : k + STRIP, :].astype(jnp.float32)
+            ee = e * e
+            ed = e * (dy * gain[k : k + STRIP])
+            sq = sq + ee[:8] + ee[8:]
+            dot = dot + ed[:8] + ed[8:]
     sub = iota((8, LANES), 0)
     halves = []
     for total in (sq, dot):
@@ -84,6 +110,7 @@
 def rows_kernel(shards, capacity, e_ref, dy_ref, gain_ref, stats_ref, owner_ref, row_ref, out_ref, rows_ref, part_ref):
     width, tokens = e_ref.shape
     padded = out_ref.shape[1]
+    position = position_of(owner_ref[...], shards, capacity)
     gain = column_of(gain_ref[...])
     pair = jnp.sum(stats_ref[...], axis=0)
     sq = jnp.concatenate([pair[s : s + 1, :LANES] for s in range(8)], axis=1)
@@ -118,14 +145,13 @@
         pieces.append(piece)
         fold = fold - piece
     extra = jnp.concatenate(pieces, axis=0)
-    position = position_of(owner_ref[...], shards, capacity)
-    group = 8
+    group = PICK
     chunk = group * capacity
     rows = rows_ref[...]
 
     def step(i, carry):
-        slot = iota((chunk, tokens), 0) + i * chunk
-        pick = (slot == position).astype(jnp.float32).astype(jnp.bfloat16)
+        half = chunk // 2
+        pick = jnp.concatenate([onehot_rows(position, i * chunk + h * half, half) for h in range(2)], axis=0)
         got = lax.dot_general(pick, rows, (((1,), (1,)), ((), ())), preferred_element_type=jnp.float32)
         last = got[:, padded - LANES :].reshape(group, capacity, LANES) + extra[None]
         where = pl.ds(pl.multiple_of(i * chunk, chunk), chunk)
@@ -133,7 +159,13 @@
         out_ref[where, padded - LANES :] = last.reshape(chunk, LANES).astype(jnp.bfloat16)
         return carry
 
-    lax.fori_loop(0, shards // group, step, 0)
+    lax.fori_loop(0, shards // group, step, 0, unroll=True)
+
+
+def onehot_rows(position, base, n):
+    local = (position - base).astype(jnp.float32).astype(jnp.bfloat16)
+    row = iota((n, position.shape[1]), 0).astype(jnp.float32).astype(jnp.bfloat16)
+    return jnp.where(row == local, jnp.bfloat16(1), jnp.bfloat16(0))
 
 
 def table_kernel(capacity, width, got_ref, table_ref, gain_ref, turned_ref, id_ref):
@@ -146,7 +178,8 @@
         turned_ref[...] = got_ref[...].T
         last = got_ref[:, padded - LANES :].astype(jnp.float32)
         lane = width - (padded - LANES)
-        id_ref[...] = (last[:, lane : lane + 1] * 8.0 + last[:, lane + 1 : lane + 2]).astype(jnp.int32)
+        ids = last[:, lane : lane + 1] * 8.0 + last[:, lane + 1 : lane + 2]
+        id_ref[...] = jnp.broadcast_to(ids, id_ref.shape)
         total = jnp.sum(last.reshape(slots // capacity, capacity, LANES), axis=0)
         fold = total[:8] + total[8:16] + total[16:24]
         span = padded - width - GAP
@@ -156,50 +189,80 @@
         )
         gain_ref[...] = jnp.sum(jnp.where(row_mask(width, span), spread, 0.0), axis=0, keepdims=True)
 
-    vocab = iota((slots, tile), 1) + j * tile
-    onehot = (vocab == id_ref[...]).astype(jnp.float32).astype(jnp.bfloat16)
-    table_ref[...] = jnp.dot(
-        turned_ref[:width, :], onehot, preferred_element_type=jnp.float32
-    ).astype(jnp.bfloat16)
+    sub_tile = min(tile, 256)
+    for t in range(tile // sub_tile):
+        base = (j * tile + t * sub_tile).astype(jnp.float32)
+        local = (id_ref[...] - base).astype(jnp.bfloat16)
+        parts = []
+        for q in range(sub_tile // LANES):
+            lane = (iota((slots, LANES), 1) + q * LANES).astype(jnp.float32).astype(jnp.bfloat16)
+            parts.append(jnp.where(local == lane, jnp.bfloat16(1), jnp.bfloat16(0)))
+        onehot = jnp.concatenate(parts, axis=1)
+        table_ref[:, t * sub_tile : (t + 1) * sub_tile] = jnp.dot(
+            turned_ref[:width, :], onehot, preferred_element_type=jnp.float32
+        ).astype(jnp.bfloat16)
+
+
+def stats_call(e, dy, gain, sections):
+    width, tokens = e.shape
+    return pl.pallas_call(
+        stats_kernel,
+        in_specs=[pl.BlockSpec(memory_space=pltpu.HBM)] * 3,
+        out_shape=jax.ShapeDtypeStruct((sections, 8, 2 * LANES), jnp.float32),
+        scratch_shapes=[
+            pltpu.VMEM((width, tokens), e.dtype),
+            pltpu.VMEM((width, tokens), dy.dtype),
+            pltpu.VMEM((1, width), jnp.float32),
+            pltpu.SemaphoreType.DMA((LOADS, 2)),
+            pltpu.SemaphoreType.DMA,
+        ],
+        compiler_params=pltpu.CompilerParams(vmem_limit_bytes=FULL_VMEM),
+    )(e, dy, gain)
+
+
+def rows_call(e, dy, gain, stats, owner, row, shards, capacity):
+    width, tokens = e.shape
+    padded = -(-width // LANES) * LANES
+    return pl.pallas_call(
+        lambda *refs: rows_kernel(shards, capacity, *refs),
+        in_specs=[pl.BlockSpec(memory_space=pltpu.VMEM)] * 6,
+        out_shape=jax.ShapeDtypeStruct((shards * capacity, padded), jnp.bfloat16),
+        scratch_shapes=[
+            pltpu.VMEM((padded, tokens), jnp.bfloat16),
+            pltpu.VMEM((width, LANES), jnp.float32),
+        ],
+        compiler_params=pltpu.CompilerParams(vmem_limit_bytes=VMEM_LIMIT),
+    )(e, dy, gain, stats, owner, row)
+
+
+def table_call(got, capacity, width, vocab_dev):
+    slots, padded = got.shape
+    return pl.pallas_call(
+        lambda *refs: table_kernel(capacity, width, *refs),
+        grid=(pl.cdiv(vocab_dev, TILE),),
+        in_specs=[pl.BlockSpec(memory_space=pltpu.VMEM)],
+        out_specs=[pl.BlockSpec((width, TILE), lambda j: (0, j)), pl.BlockSpec((1, width), lambda j: (0, 0))],
+        out_shape=[
+            jax.ShapeDtypeStruct((width, vocab_dev), jnp.bfloat16),
+            jax.ShapeDtypeStruct((1, width), jnp.float32),
+        ],
+        scratch_shapes=[pltpu.VMEM((padded, slots), jnp.bfloat16), pltpu.VMEM((slots, LANES), jnp.float32)],
+        compiler_params=pltpu.CompilerParams(vmem_limit_bytes=VMEM_LIMIT),
+    )(got)
 
 
 def on_device(emb_rows, grad_normed, norm_gain, owner_shard, row_in_shard):
     tokens, width = emb_rows.shape
     sections, shards = lax.axis_size("section"), lax.axis_size("dp")
     capacity = 3 * tokens // (2 * shards)
-    vocab_dev = VOCAB // shards
-    padded = -(-width // LANES) * LANES
-    slots = shards * capacity
     e, dy = emb_rows.T, grad_normed.T
     gain = norm_gain.reshape(1, width)
     owner, row = owner_shard.reshape(1, tokens), row_in_shard.reshape(1, tokens)
-    params = pltpu.CompilerParams(vmem_limit_bytes=VMEM_LIMIT)
-    stats = pl.pallas_call(
-        stats_kernel,
-        out_shape=jax.ShapeDtypeStruct((sections, 8, 2 * LANES), jnp.float32),
-        compiler_params=params,
-    )(e, dy, gain)
-    stats = lax.all_to_all(stats, "section", 0, 0, tiled=True)
-    message = pl.pallas_call(
-        lambda *refs: rows_kernel(shards, capacity, *refs),
-        out_shape=jax.ShapeDtypeStruct((slots, padded), jnp.bfloat16),
-        scratch_shapes=[pltpu.VMEM((padded, tokens), jnp.bfloat16), pltpu.VMEM((width, LANES), jnp.float32)],
-        compiler_params=params,
-    )(e, dy, gain, stats, owner, row)
-    got = lax.all_to_all(message.reshape(shards, capacity, padded), "dp", 0, 0, tiled=True)
-    tile = 512
-    table, gain_gradient = pl.pallas_call(
-        lambda *refs: table_kernel(capacity, width, *refs),
-        grid=(pl.cdiv(vocab_dev, tile),),
-        in_specs=[pl.BlockSpec((slots, padded), lambda j: (0, 0))],
-        out_specs=[pl.BlockSpec((width, tile), lambda j: (0, j)), pl.BlockSpec((1, width), lambda j: (0, 0))],
-        out_shape=[
-            jax.ShapeDtypeStruct((width, vocab_dev), jnp.bfloat16),
-            jax.ShapeDtypeStruct((1, width), jnp.float32),
-        ],
-        scratch_shapes=[pltpu.VMEM((padded, slots), jnp.bfloat16), pltpu.VMEM((slots, 1), jnp.int32)],
-        compiler_params=params,
-    )(got.reshape(slots, padded))
+    stats = lax.all_to_all(stats_call(e, dy, gain, sections), "section", 0, 0, tiled=True)
+    message = rows_call(e, dy, gain, stats, owner, row, shards, capacity)
+    message = message.reshape(shards, capacity, -1)
+    got = lax.all_to_all(message, "dp", 0, 0, tiled=True)
+    table, gain_gradient = table_call(got.reshape(shards * capacity, -1), capacity, width, VOCAB // shards)
     return (table.T, gain_gradient.reshape(width))
 
 

time: 96.8 us -> 93.6 us (0.967)
  local copies, waits for them, and re-layouts: 3.05 us -> 0.02 us
    unnamed x10, local copies, waits for them, and re-layouts: 3.05 us -> 0.02 us
where the time goes in v2:
time: 93.6 us; the launch traced here: 93.4 us
  blocking collectives  82.7 us (88%)
  Pallas kernels  9.99 us (11%)
    all_to_all x1, blocking collectives, on_device(): got = lax.all_to_all(message, 'dp', 0, 0, tiled=True)  66.3 us
    all_to_all x1, blocking collectives, on_device(): lax.all_to_all(stats_call(e, dy, gain, sections), 'section', 0, 0, tiled=...  16.4 us
    pallas_call x1, Pallas kernels, table_call(): pl.pallas_call(lambda *refs: table_kernel(capacity, width, *refs), grid=(...  4.92 us
    pallas_call x1, Pallas kernels, rows_call(): pl.pallas_call(lambda *refs: rows_kernel(shards, capacity, *refs), in_spe...  2.6 us
    pallas_call x1, Pallas kernels, stats_call(): pl.pallas_call(stats_kernel, in_specs=[pl.BlockSpec(memory_space=pltpu.HB...  2.47 us

profile of v2, /device:TPU:6, one launch (start us, length us, event | category | flops | bytes accessed | tf_op | source)
XLA Modules:
  0.0 93.4 jit_solution(5632246331283591015)
XLA Ops:
  0.6 0.0 copy-start.2
  0.6 0.0 copy-start.1
  0.7 0.0 copy-start
  0.7 0.0 copy-start.4
  0.7 0.0 copy-start.3
  0.7 2.5 %shard_map.68 = f32[16,8,256]{2,1,0:T(8,128)} custom-call(bf16[448,1024]{1,0:T(8,128)(2,1)} %bitcast.11, bf16[448,1024]{1,0:T(8,128)(2,1)} %bitcast.13, f32[1,448]{1,0:T(1,128)} %bitcast.15), custom_call_target="tpu_custom_call" | custom-call | tf_op jit(solution)/shard_map/pallas_call | solution.py:208
  3.2 16.4 %all_to_all.10.refs_3_ = f32[16,8,256]{2,1,0:T(8,128)S(1)} all-to-all(f32[16,8,256]{2,1,0:T(8,128)} %shard_map.68), channel_id=1, replica_groups=mesh['section'=16,'dp'=64] {'section'}, dimensions={0} | all-to-all | bytes 262144 | tf_op jit(solution)/shard_map/all_to_all | solution.py:261
  19.6 0.0 copy-done.2
  19.6 0.0 copy-done.1
  19.6 0.0 copy-done
  19.6 0.0 copy-done.4
  19.6 0.0 copy-done.3
  19.6 2.6 %shard_map.69 = bf16[1536,512]{1,0:T(8,128)(2,1)S(1)} custom-call(bf16[448,1024]{1,0:T(8,128)(2,1)S(1)} %bitcast.12, bf16[448,1024]{1,0:T(8,128)(2,1)S(1)} %bitcast.14, f32[1,448]{1,0:T(1,128)S(1)} %bitcast.16, f32[16,8,256]{2,1,0:T(8,128)S(1)} %all_to_all.10.refs_3_, s32[1,1024]{1,0:T(1,128)S(1)} %bitcast.17, s32[1,1024]{1,0:T(1,128)S(1)} %bitcast.18), custom_call_target="tpu_custom_call" | custom-call | tf_op jit(solution)/shard_map/pallas_call | solution.py:226
  22.2 66.3 %all_to_all.11 = bf16[64,24,512]{2,1,0:T(8,128)(2,1)S(1)} all-to-all(bf16[64,24,512]{2,1,0:T(8,128)(2,1)S(1)} %bitcast.10), channel_id=1, replica_groups=mesh['section'=16,'dp'=64] {'dp'}, dimensions={0} | all-to-all | bytes 3145728 | tf_op jit(solution)/shard_map/all_to_all | solution.py:264
  88.5 4.9 %shard_map.70 = (bf16[448,2020]{1,0:T(8,128)(2,1)}, f32[1,448]{1,0:T(1,128)}) custom-call(bf16[1536,512]{1,0:T(8,128)(2,1)S(1)} %bitcast.9), custom_call_target="tpu_custom_call" | custom-call | tf_op jit(solution)/shard_map/pallas_call | solution.py:240
Async XLA Ops:
  0.6 18.9 %copy-start.2 = (f32[448]{0:T(512)S(1)}, f32[448]{0:T(512)}, u32[]{:S(2)}) copy-start(f32[448]{0:T(512)} %param.7) | copy-start | bytes 5380
  0.6 18.9 %copy-start.1 = (bf16[1024,448]{0,1:T(8,128)(2,1)S(1)}, bf16[1024,448]{0,1:T(8,128)(2,1)}, u32[]{:S(2)}) copy-start(bf16[1024,448]{0,1:T(8,128)(2,1)} %param.6) | copy-start | bytes 2752516
  0.7 18.9 %copy-start = (bf16[1024,448]{0,1:T(8,128)(2,1)S(1)}, bf16[1024,448]{0,1:T(8,128)(2,1)}, u32[]{:S(2)}) copy-start(bf16[1024,448]{0,1:T(8,128)(2,1)} %param.5) | copy-start | bytes 2752516
  0.7 18.9 %copy-start.4 = (s32[1024,1]{0,1:T(1,128)S(1)}, s32[1024,1]{0,1:T(1,128)}, u32[]{:S(2)}) copy-start(s32[1024,1]{0,1:T(1,128)} %param.9) | copy-start | bytes 12292
  0.7 18.9 %copy-start.3 = (s32[1024,1]{0,1:T(1,128)S(1)}, s32[1024,1]{0,1:T(1,128)}, u32[]{:S(2)}) copy-start(s32[1024,1]{0,1:T(1,128)} %param.8) | copy-start | bytes 12292

commit v3 on v2

--- a/solution.py
+++ b/solution.py
@@ -10,8 +10,9 @@
 EPS = 1e-06
 LANES = 128
 STRIP = 16
-PIECES = 3
-GAP = 8
+HALF = LANES // 2
+LEVELS = 240 * 128
+SCALE_LANE = HALF + 48
 LOADS = 2
 VMEM_LIMIT = 40 * 1024 * 1024
 FULL_VMEM = 62 * 1024 * 1024
@@ -28,19 +29,44 @@
     return jnp.sum(jnp.where(iota((n, n), 0) == iota((n, n), 1), row, 0.0), axis=1, keepdims=True)
 
 
-def fold_mask(n, width, first, lane_dim):
+def fold_mask(n, lane_dim):
     shape = (n, LANES) if lane_dim == 1 else (LANES, n)
-    lane = iota(shape, lane_dim) - first
+    lane = iota(shape, lane_dim) - HALF
     feature = iota(shape, 1 - lane_dim)
     hit = feature == lane
-    for r in range(1, n // width):
-        hit = hit | (feature - r * width == lane)
-    return hit & (lane >= 0) & (lane < width)
-
-
-def row_mask(n, width):
-    offset = iota((8, n), 1) - iota((8, n), 0) * width
-    return (offset >= 0) & (offset < width)
+    for r in range(1, n // HALF):
+        hit = hit | (feature - r * HALF == lane)
+    return hit & (lane >= 0)
+
+
+def row_mask(n):
+    offset = iota((8, n), 1) - (iota((8, n), 0) - 1) * HALF
+    return (offset >= 0) & (offset < HALF)
+
+
+def encode(q):
+    size = jnp.abs(q)
+    binade = jnp.floor(size * (1.0 / 128.0))
+    value = 1.0 + (size - binade * 128.0) * (1.0 / 128.0)
+    value = value * 2.0**-120
+    for bit in (128, 64, 32, 16, 8, 4, 2, 1):
+        take = binade >= bit
+        binade = jnp.where(take, binade - bit, binade)
+        for _ in range(2 if bit == 128 else 1):
+            value = jnp.where(take, value * 2.0 ** min(bit, 64), value)
+    return jnp.where(q < 0, -value, value)
+
+
+def decode(code):
+    value = jnp.abs(code)
+    size = jnp.zeros_like(value)
+    for bit in (128, 64, 32, 16, 8, 4, 2, 1):
+        take = value >= 2.0 ** (bit - 120)
+        size = jnp.where(take, size + bit * 128.0, size)
+        for _ in range(2 if bit == 128 else 1):
+            value = jnp.where(take, value * 2.0 ** -min(bit, 64), value)
+    size = size + (value * 2.0**120 * 128.0 - 128.0)
+    return jnp.where(code < 0, -size, size)
 
 
 def copies_of(pairs, sems, parts):
@@ -89,7 +115,7 @@
     out_ref[...] = jnp.broadcast_to(pair[None], out_ref.shape)
 
 
-def position_of(owner, shards, capacity):
+def ranks_of(owner, shards):
     tokens = owner.shape[1]
     blocks = tokens // LANES
     marks = (iota((shards, tokens), 0) == owner).astype(jnp.float32)
@@ -103,14 +129,26 @@
         rows = slice(b * shards, (b + 1) * shards)
         ranks.append(jnp.sum(stacked[rows] * (before[rows] + start), axis=0, keepdims=True))
         start = start + totals[rows]
-    rank = jnp.concatenate(ranks, axis=1)
-    return owner * capacity + rank.astype(jnp.int32)
+    rank = jnp.concatenate(ranks, axis=1).astype(jnp.int32)
+    return marks, rank
 
 
 def rows_kernel(shards, capacity, e_ref, dy_ref, gain_ref, stats_ref, owner_ref, row_ref, out_ref, rows_ref, part_ref):
     width, tokens = e_ref.shape
-    padded = out_ref.shape[1]
-    position = position_of(owner_ref[...], shards, capacity)
+    padded = rows_ref.shape[0]
+    owner = owner_ref[...]
+    marks, rank = ranks_of(owner, shards)
+    position = owner * capacity + rank
+    ids = row_ref[...]
+    spot = iota((LANES, tokens), 0) - HALF
+    id_rows = jnp.zeros((shards, LANES), jnp.float32)
+    for part, first in ((ids >> 3, 0), (ids & 7, capacity)):
+        id_rows = id_rows + lax.dot_general(
+            (marks * part.astype(jnp.float32)).astype(jnp.bfloat16),
+            (spot == rank + first).astype(jnp.float32).astype(jnp.bfloat16),
+            (((1,), (1,)), ((), ())),
+            preferred_element_type=jnp.float32,
+        )
     gain = column_of(gain_ref[...])
     pair = jnp.sum(stats_ref[...], axis=0)
     sq = jnp.concatenate([pair[s : s + 1, :LANES] for s in range(8)], axis=1)
@@ -126,40 +164,36 @@
         for s in range(1, tokens // LANES):
             part = part + term[:, s * LANES : (s + 1) * LANES]
         part_ref[k : k + STRIP, :] = part
-    ids = row_ref[...]
-    sub = iota((padded - width, tokens), 0)
-    rows_ref[width:, :] = jnp.where(
-        sub == 0, ids >> 3, jnp.where(sub == 1, ids & 7, 0)
-    ).astype(jnp.float32).astype(jnp.bfloat16)
-    span = padded - width - GAP
-    first = LANES - span
+    rows_ref[width:, :] = jnp.zeros((padded - width, tokens), jnp.bfloat16)
     partial = jnp.sum(part_ref[...], axis=1, keepdims=True)
-    spread = jnp.where(fold_mask(width, span, first, 1), partial, 0.0)
+    scale = jnp.maximum(jnp.max(jnp.abs(partial), axis=0, keepdims=True), 1e-30)
+    steps = jnp.floor(partial * ((LEVELS - 1) / scale) + 0.5)
+    steps = jnp.clip(steps, -(LEVELS - 1.0), LEVELS - 1.0)
     fold = jnp.dot(
-        row_mask(width, span).astype(jnp.float32), spread,
+        row_mask(width).astype(jnp.float32), jnp.where(fold_mask(width, 1), steps, 0.0),
         precision=lax.Precision.HIGHEST, preferred_element_type=jnp.float32,
     )
-    pieces = []
-    for _ in range(PIECES):
-        piece = fold.astype(jnp.bfloat16).astype(jnp.float32)
-        pieces.append(piece)
-        fold = fold - piece
-    extra = jnp.concatenate(pieces, axis=0)
-    group = PICK
-    chunk = group * capacity
+    sub, lane = iota((8, LANES), 0), iota((8, LANES), 1)
+    extra = jnp.where((sub > 0) & (lane >= HALF), encode(jnp.floor(fold + 0.5)), 0.0)
+    for n in range(3):
+        piece = scale.astype(jnp.bfloat16).astype(jnp.float32)
+        extra = jnp.where((sub == 0) & (lane == SCALE_LANE + n), piece, extra)
+        scale = scale - piece
     rows = rows_ref[...]
-
-    def step(i, carry):
-        half = chunk // 2
-        pick = jnp.concatenate([onehot_rows(position, i * chunk + h * half, half) for h in range(2)], axis=0)
+    for first in range(0, shards, PICK):
+        half = PICK // 2 * capacity
+        pick = jnp.concatenate([onehot_rows(position, first * capacity + h * half, half) for h in range(2)], axis=0)
         got = lax.dot_general(pick, rows, (((1,), (1,)), ((), ())), preferred_element_type=jnp.float32)
-        last = got[:, padded - LANES :].reshape(group, capacity, LANES) + extra[None]
-        where = pl.ds(pl.multiple_of(i * chunk, chunk), chunk)
-        out_ref[where, : padded - LANES] = got[:, : padded - LANES].astype(jnp.bfloat16)
-        out_ref[where, padded - LANES :] = last.reshape(chunk, LANES).astype(jnp.bfloat16)
-        return carry
-
-    lax.fori_loop(0, shards // group, step, 0, unroll=True)
+        pieces = []
+        for n in range(PICK):
+            mine = got[n * capacity : (n + 1) * capacity]
+            pieces += [mine[:, k : k + LANES] for k in range(0, padded - LANES, LANES)]
+            last = mine[:, padded - LANES :]
+            shard = first + n
+            pieces.append(last[:8] + pltpu.roll(last[16:], HALF, 1))
+            pieces.append(last[8:16] + jnp.where(sub == 0, extra + id_rows[shard : shard + 1], extra))
+        size = out_ref.shape[0] // shards * PICK
+        out_ref[first // PICK * size : (first // PICK + 1) * size] = jnp.concatenate(pieces, axis=0).astype(jnp.bfloat16)
 
 
 def onehot_rows(position, base, n):
@@ -168,26 +202,35 @@
     return jnp.where(row == local, jnp.bfloat16(1), jnp.bfloat16(0))
 
 
-def table_kernel(capacity, width, got_ref, table_ref, gain_ref, turned_ref, id_ref):
-    slots, padded = got_ref.shape
-    tile = table_ref.shape[1]
+def table_kernel(shards, capacity, got_ref, table_ref, gain_ref, turned_ref, id_ref):
+    width, tile = table_ref.shape
+    slots = shards * capacity
     j = pl.program_id(0)
 
     @pl.when(j == 0)
     def _():
-        turned_ref[...] = got_ref[...].T
-        last = got_ref[:, padded - LANES :].astype(jnp.float32)
-        lane = width - (padded - LANES)
-        ids = last[:, lane : lane + 1] * 8.0 + last[:, lane + 1 : lane + 2]
+        got = got_ref[...].astype(jnp.float32).reshape(shards, -1, LANES)
+        full = width // LANES
+        for k in range(full):
+            block = got[:, k * capacity : (k + 1) * capacity].reshape(slots, LANES)
+            turned_ref[k * LANES : (k + 1) * LANES] = block.astype(jnp.bfloat16).T
+        last = got[:, full * capacity :]
+        block = jnp.concatenate([last, pltpu.roll(last[:, :8].reshape(shards * 8, LANES), HALF, 1).reshape(shards, 8, LANES)], axis=1)
+        turned_ref[full * LANES :] = block.reshape(slots, LANES).astype(jnp.bfloat16).T[:HALF]
+        extra = last[:, 8:]
+        spot, lane = iota((capacity, LANES), 0), iota((capacity, LANES), 1) - HALF
+        weight = jnp.where(lane == spot, 8.0, jnp.where(lane == spot + capacity, 1.0, 0.0))
+        ids = jnp.sum(extra[:, :1] * weight[None], axis=2, keepdims=True).reshape(slots, 1)
         id_ref[...] = jnp.broadcast_to(ids, id_ref.shape)
-        total = jnp.sum(last.reshape(slots // capacity, capacity, LANES), axis=0)
-        fold = total[:8] + total[8:16] + total[16:24]
-        span = padded - width - GAP
+        at = iota((1, LANES), 1)
+        scale = jnp.where((at >= SCALE_LANE) & (at < SCALE_LANE + 3), extra[:, 0], 0.0)
+        scale = jnp.sum(scale, axis=1, keepdims=True) * (1.0 / (LEVELS - 1))
+        fold = jnp.sum(decode(extra) * scale[:, :, None], axis=0)
         spread = jnp.dot(
-            fold, fold_mask(width, span, LANES - span, 0).astype(jnp.float32),
+            fold, fold_mask(width, 0).astype(jnp.float32),
             precision=lax.Precision.HIGHEST, preferred_element_type=jnp.float32,
         )
-        gain_ref[...] = jnp.sum(jnp.where(row_mask(width, span), spread, 0.0), axis=0, keepdims=True)
+        gain_ref[...] = jnp.sum(jnp.where(row_mask(width), spread, 0.0), axis=0, keepdims=True)
 
     sub_tile = min(tile, 256)
     for t in range(tile // sub_tile):
@@ -199,7 +242,7 @@
             parts.append(jnp.where(local == lane, jnp.bfloat16(1), jnp.bfloat16(0)))
         onehot = jnp.concatenate(parts, axis=1)
         table_ref[:, t * sub_tile : (t + 1) * sub_tile] = jnp.dot(
-            turned_ref[:width, :], onehot, preferred_element_type=jnp.float32
+            turned_ref[...], onehot, preferred_element_type=jnp.float32
         ).astype(jnp.bfloat16)
 
 
@@ -223,10 +266,11 @@
 def rows_call(e, dy, gain, stats, owner, row, shards, capacity):
     width, tokens = e.shape
     padded = -(-width // LANES) * LANES
+    message = width // LANES * capacity + 16
     return pl.pallas_call(
         lambda *refs: rows_kernel(shards, capacity, *refs),
         in_specs=[pl.BlockSpec(memory_space=pltpu.VMEM)] * 6,
-        out_shape=jax.ShapeDtypeStruct((shards * capacity, padded), jnp.bfloat16),
+        out_shape=jax.ShapeDtypeStruct((shards * message, LANES), jnp.bfloat16),
         scratch_shapes=[
             pltpu.VMEM((padded, tokens), jnp.bfloat16),
             pltpu.VMEM((width, LANES), jnp.float32),
@@ -235,10 +279,10 @@
     )(e, dy, gain, stats, owner, row)
 
 
-def table_call(got, capacity, width, vocab_dev):
-    slots, padded = got.shape
+def table_call(got, shards, capacity, width, vocab_dev):
+    slots = shards * capacity
     return pl.pallas_call(
-        lambda *refs: table_kernel(capacity, width, *refs),
+        lambda *refs: table_kernel(shards, capacity, *refs),
         grid=(pl.cdiv(vocab_dev, TILE),),
         in_specs=[pl.BlockSpec(memory_space=pltpu.VMEM)],
         out_specs=[pl.BlockSpec((width, TILE), lambda j: (0, j)), pl.BlockSpec((1, width), lambda j: (0, 0))],
@@ -246,7 +290,7 @@
             jax.ShapeDtypeStruct((width, vocab_dev), jnp.bfloat16),
             jax.ShapeDtypeStruct((1, width), jnp.float32),
         ],
-        scratch_shapes=[pltpu.VMEM((padded, slots), jnp.bfloat16), pltpu.VMEM((slots, LANES), jnp.float32)],
+        scratch_shapes=[pltpu.VMEM((width, slots), jnp.bfloat16), pltpu.VMEM((slots, LANES), jnp.float32)],
         compiler_params=pltpu.CompilerParams(vmem_limit_bytes=VMEM_LIMIT),
     )(got)
 
@@ -260,9 +304,9 @@
     owner, row = owner_shard.reshape(1, tokens), row_in_shard.reshape(1, tokens)
     stats = lax.all_to_all(stats_call(e, dy, gain, sections), "section", 0, 0, tiled=True)
     message = rows_call(e, dy, gain, stats, owner, row, shards, capacity)
-    message = message.reshape(shards, capacity, -1)
+    message = message.reshape(shards, -1, LANES)
     got = lax.all_to_all(message, "dp", 0, 0, tiled=True)
-    table, gain_gradient = table_call(got.reshape(shards * capacity, -1), capacity, width, VOCAB // shards)
+    table, gain_gradient = table_call(got.reshape(-1, LANES), shards, capacity, width, VOCAB // shards)
     return (table.T, gain_gradient.reshape(width))
 
 

time: 93.6 us -> 90.7 us (0.969)
  blocking collectives: 82.7 us -> 79.2 us
    all_to_all x1, blocking collectives: 66.3 us -> 62.8 us  [on_device(): got = lax.all_to_all(message, 'dp', 0, 0, tiled=True)]
where the time goes in v3:
time: 90.7 us; the launch traced here: 90.5 us
  blocking collectives  79.2 us (87%)
  Pallas kernels  10.6 us (12%)
    all_to_all x1, blocking collectives, on_device(): got = lax.all_to_all(message, 'dp', 0, 0, tiled=True)  62.8 us
    all_to_all x1, blocking collectives, on_device(): lax.all_to_all(stats_call(e, dy, gain, sections), 'section', 0, 0, tiled=...  16.4 us
    pallas_call x1, Pallas kernels, table_call(): pl.pallas_call(lambda *refs: table_kernel(shards, capacity, *refs), grid=...  5.22 us
    pallas_call x1, Pallas kernels, rows_call(): pl.pallas_call(lambda *refs: rows_kernel(shards, capacity, *refs), in_spe...  2.91 us
    pallas_call x1, Pallas kernels, stats_call(): pl.pallas_call(stats_kernel, in_specs=[pl.BlockSpec(memory_space=pltpu.HB...  2.47 us

profile of v3, /device:TPU:6, one launch (start us, length us, event | category | flops | bytes accessed | tf_op | source)
XLA Modules:
  0.0 90.5 jit_solution(16692441213527806569)
XLA Ops:
  0.6 0.0 copy-start.2
  0.6 0.0 copy-start.1
  0.7 0.0 copy-start
  0.7 0.0 copy-start.4
  0.7 0.0 copy-start.3
  0.7 2.5 %shard_map.68 = f32[16,8,256]{2,1,0:T(8,128)} custom-call(bf16[448,1024]{1,0:T(8,128)(2,1)} %bitcast.11, bf16[448,1024]{1,0:T(8,128)(2,1)} %bitcast.13, f32[1,448]{1,0:T(1,128)} %bitcast.15), custom_call_target="tpu_custom_call" | custom-call | tf_op jit(solution)/shard_map/pallas_call | solution.py:251
  3.2 16.4 %all_to_all.10.refs_3_ = f32[16,8,256]{2,1,0:T(8,128)S(1)} all-to-all(f32[16,8,256]{2,1,0:T(8,128)} %shard_map.68), channel_id=1, replica_groups=mesh['section'=16,'dp'=64] {'section'}, dimensions={0} | all-to-all | bytes 262144 | tf_op jit(solution)/shard_map/all_to_all | solution.py:305
  19.6 0.0 copy-done.2
  19.6 0.0 copy-done.1
  19.6 0.0 copy-done
  19.6 0.0 copy-done.4
  19.6 0.0 copy-done.3
  19.6 2.9 %shard_map.69 = bf16[5632,128]{1,0:T(8,128)(2,1)S(1)} custom-call(bf16[448,1024]{1,0:T(8,128)(2,1)S(1)} %bitcast.12, bf16[448,1024]{1,0:T(8,128)(2,1)S(1)} %bitcast.14, f32[1,448]{1,0:T(1,128)S(1)} %bitcast.16, f32[16,8,256]{2,1,0:T(8,128)S(1)} %all_to_all.10.refs_3_, s32[1,1024]{1,0:T(1,128)S(1)} %bitcast.17, s32[1,1024]{1,0:T(1,128)S(1)} %bitcast.18), custom_call_target="tpu_custom_call" | custom-call | tf_op jit(solution)/shard_map/pallas_call | solution.py:270
  22.5 62.8 %all_to_all.11 = bf16[64,88,128]{2,1,0:T(8,128)(2,1)S(1)} all-to-all(bf16[64,88,128]{2,1,0:T(8,128)(2,1)S(1)} %bitcast.10), channel_id=1, replica_groups=mesh['section'=16,'dp'=64] {'dp'}, dimensions={0} | all-to-all | bytes 2883584 | tf_op jit(solution)/shard_map/all_to_all | solution.py:308
  85.3 5.2 %shard_map.70 = (bf16[448,2020]{1,0:T(8,128)(2,1)}, f32[1,448]{1,0:T(1,128)}) custom-call(bf16[5632,128]{1,0:T(8,128)(2,1)S(1)} %bitcast.9), custom_call_target="tpu_custom_call" | custom-call | tf_op jit(solution)/shard_map/pallas_call | solution.py:284
Async XLA Ops:
  0.6 18.9 %copy-start.2 = (f32[448]{0:T(512)S(1)}, f32[448]{0:T(512)}, u32[]{:S(2)}) copy-start(f32[448]{0:T(512)} %param.7) | copy-start | bytes 5380
  0.6 18.9 %copy-start.1 = (bf16[1024,448]{0,1:T(8,128)(2,1)S(1)}, bf16[1024,448]{0,1:T(8,128)(2,1)}, u32[]{:S(2)}) copy-start(bf16[1024,448]{0,1:T(8,128)(2,1)} %param.6) | copy-start | bytes 2752516
  0.7 18.9 %copy-start = (bf16[1024,448]{0,1:T(8,128)(2,1)S(1)}, bf16[1024,448]{0,1:T(8,128)(2,1)}, u32[]{:S(2)}) copy-start(bf16[1024,448]{0,1:T(8,128)(2,1)} %param.5) | copy-start | bytes 2752516
  0.7 18.9 %copy-start.4 = (s32[1024,1]{0,1:T(1,128)S(1)}, s32[1024,1]{0,1:T(1,128)}, u32[]{:S(2)}) copy-start(s32[1024,1]{0,1:T(1,128)} %param.9) | copy-start | bytes 12292
  0.7 18.9 %copy-start.3 = (s32[1024,1]{0,1:T(1,128)S(1)}, s32[1024,1]{0,1:T(1,128)}, u32[]{:S(2)}) copy-start(s32[1024,1]{0,1:T(1,128)} %param.8) | copy-start | bytes 12292

commit v4 on v3

--- a/solution.py
+++ b/solution.py
@@ -207,6 +207,20 @@
     slots = shards * capacity
     j = pl.program_id(0)
 
+    def sums():
+        sub_tile = min(tile, 256)
+        for t in range(tile // sub_tile):
+            base = (j * tile + t * sub_tile).astype(jnp.float32)
+            local = (id_ref[...] - base).astype(jnp.bfloat16)
+            parts = []
+            for q in range(sub_tile // LANES):
+                lane = (iota((slots, LANES), 1) + q * LANES).astype(jnp.float32).astype(jnp.bfloat16)
+                parts.append(jnp.where(local == lane, jnp.bfloat16(1), jnp.bfloat16(0)))
+            onehot = jnp.concatenate(parts, axis=1)
+            table_ref[:, t * sub_tile : (t + 1) * sub_tile] = jnp.dot(
+                turned_ref[...], onehot, preferred_element_type=jnp.float32
+            ).astype(jnp.bfloat16)
+
     @pl.when(j == 0)
     def _():
         got = got_ref[...].astype(jnp.float32).reshape(shards, -1, LANES)
@@ -222,6 +236,7 @@
         weight = jnp.where(lane == spot, 8.0, jnp.where(lane == spot + capacity, 1.0, 0.0))
         ids = jnp.sum(extra[:, :1] * weight[None], axis=2, keepdims=True).reshape(slots, 1)
         id_ref[...] = jnp.broadcast_to(ids, id_ref.shape)
+        sums()
         at = iota((1, LANES), 1)
         scale = jnp.where((at >= SCALE_LANE) & (at < SCALE_LANE + 3), extra[:, 0], 0.0)
         scale = jnp.sum(scale, axis=1, keepdims=True) * (1.0 / (LEVELS - 1))
@@ -232,18 +247,9 @@
         )
         gain_ref[...] = jnp.sum(jnp.where(row_mask(width), spread, 0.0), axis=0, keepdims=True)
 
-    sub_tile = min(tile, 256)
-    for t in range(tile // sub_tile):
-        base = (j * tile + t * sub_tile).astype(jnp.float32)
-        local = (id_ref[...] - base).astype(jnp.bfloat16)
-        parts = []
-        for q in range(sub_tile // LANES):
-            lane = (iota((slots, LANES), 1) + q * LANES).astype(jnp.float32).astype(jnp.bfloat16)
-            parts.append(jnp.where(local == lane, jnp.bfloat16(1), jnp.bfloat16(0)))
-        onehot = jnp.concatenate(parts, axis=1)
-        table_ref[:, t * sub_tile : (t + 1) * sub_tile] = jnp.dot(
-            turned_ref[...], onehot, preferred_element_type=jnp.float32
-        ).astype(jnp.bfloat16)
+    @pl.when(j > 0)
+    def _():
+        sums()
 
 
 def stats_call(e, dy, gain, sections):
@@ -251,7 +257,7 @@
     return pl.pallas_call(
         stats_kernel,
         in_specs=[pl.BlockSpec(memory_space=pltpu.HBM)] * 3,
-        out_shape=jax.ShapeDtypeStruct((sections, 8, 2 * LANES), jnp.float32),
+        out_shape=pltpu.VMEM((sections, 8, 2 * LANES), jnp.float32),
         scratch_shapes=[
             pltpu.VMEM((width, tokens), e.dtype),
             pltpu.VMEM((width, tokens), dy.dtype),

time: 90.7 us -> 89.3 us (0.985)
  Pallas kernels: 10.6 us -> 9.3 us
where the time goes in v4:
time: 89.3 us; the launch traced here: 89.1 us
  blocking collectives  79.1 us (89%)
  Pallas kernels  9.3 us (10%)
    all_to_all x1, blocking collectives, on_device(): got = lax.all_to_all(message, 'dp', 0, 0, tiled=True)  62.9 us
    all_to_all x1, blocking collectives, on_device(): lax.all_to_all(stats_call(e, dy, gain, sections), 'section', 0, 0, tiled=...  16.2 us
    pallas_call x1, Pallas kernels, table_call(): pl.pallas_call(lambda *refs: table_kernel(shards, capacity, *refs), grid=...  4.58 us
    pallas_call x1, Pallas kernels, rows_call(): pl.pallas_call(lambda *refs: rows_kernel(shards, capacity, *refs), in_spe...  2.91 us
    pallas_call x1, Pallas kernels, stats_call(): pl.pallas_call(stats_kernel, in_specs=[pl.BlockSpec(memory_space=pltpu.HB...  1.81 us

profile of v4, /device:TPU:6, one launch (start us, length us, event | category | flops | bytes accessed | tf_op | source)
XLA Modules:
  0.0 89.1 jit_solution(12787122170277478201)
XLA Ops:
  0.6 0.0 copy-start.2
  0.6 0.0 copy-start.1
  0.7 0.0 copy-start
  0.7 0.0 copy-start.4
  0.7 0.0 copy-start.3
  0.7 1.8 %shard_map.68 = f32[16,8,256]{2,1,0:T(8,128)S(1)} custom-call(bf16[448,1024]{1,0:T(8,128)(2,1)} %bitcast.11, bf16[448,1024]{1,0:T(8,128)(2,1)} %bitcast.13, f32[1,448]{1,0:T(1,128)} %bitcast.15), custom_call_target="tpu_custom_call" | custom-call | tf_op jit(solution)/shard_map/pallas_call | solution.py:257
  2.5 16.2 %all_to_all.10.refs_3_ = f32[16,8,256]{2,1,0:T(8,128)S(1)} all-to-all(f32[16,8,256]{2,1,0:T(8,128)S(1)} %shard_map.68), channel_id=1, replica_groups=mesh['section'=16,'dp'=64] {'section'}, dimensions={0} | all-to-all | bytes 262144 | tf_op jit(solution)/shard_map/all_to_all | solution.py:311
  18.7 0.0 copy-done.2
  18.7 0.0 copy-done.1
  18.7 0.0 copy-done
  18.7 0.0 copy-done.4
  18.7 0.0 copy-done.3
  18.7 2.9 %shard_map.69 = bf16[5632,128]{1,0:T(8,128)(2,1)S(1)} custom-call(bf16[448,1024]{1,0:T(8,128)(2,1)S(1)} %bitcast.12, bf16[448,1024]{1,0:T(8,128)(2,1)S(1)} %bitcast.14, f32[1,448]{1,0:T(1,128)S(1)} %bitcast.16, f32[16,8,256]{2,1,0:T(8,128)S(1)} %all_to_all.10.refs_3_, s32[1,1024]{1,0:T(1,128)S(1)} %bitcast.17, s32[1,1024]{1,0:T(1,128)S(1)} %bitcast.18), custom_call_target="tpu_custom_call" | custom-call | tf_op jit(solution)/shard_map/pallas_call | solution.py:276
  21.6 62.9 %all_to_all.11 = bf16[64,88,128]{2,1,0:T(8,128)(2,1)S(1)} all-to-all(bf16[64,88,128]{2,1,0:T(8,128)(2,1)S(1)} %bitcast.10), channel_id=1, replica_groups=mesh['section'=16,'dp'=64] {'dp'}, dimensions={0} | all-to-all | bytes 2883584 | tf_op jit(solution)/shard_map/all_to_all | solution.py:314
  84.5 4.6 %shard_map.70 = (bf16[448,2020]{1,0:T(8,128)(2,1)}, f32[1,448]{1,0:T(1,128)}) custom-call(bf16[5632,128]{1,0:T(8,128)(2,1)S(1)} %bitcast.9), custom_call_target="tpu_custom_call" | custom-call | tf_op jit(solution)/shard_map/pallas_call | solution.py:290
Async XLA Ops:
  0.6 18.0 %copy-start.2 = (f32[448]{0:T(512)S(1)}, f32[448]{0:T(512)}, u32[]{:S(2)}) copy-start(f32[448]{0:T(512)} %param.7) | copy-start | bytes 5380
  0.6 18.0 %copy-start.1 = (bf16[1024,448]{0,1:T(8,128)(2,1)S(1)}, bf16[1024,448]{0,1:T(8,128)(2,1)}, u32[]{:S(2)}) copy-start(bf16[1024,448]{0,1:T(8,128)(2,1)} %param.6) | copy-start | bytes 2752516
  0.7 18.0 %copy-start = (bf16[1024,448]{0,1:T(8,128)(2,1)S(1)}, bf16[1024,448]{0,1:T(8,128)(2,1)}, u32[]{:S(2)}) copy-start(bf16[1024,448]{0,1:T(8,128)(2,1)} %param.5) | copy-start | bytes 2752516
  0.7 18.0 %copy-start.4 = (s32[1024,1]{0,1:T(1,128)S(1)}, s32[1024,1]{0,1:T(1,128)}, u32[]{:S(2)}) copy-start(s32[1024,1]{0,1:T(1,128)} %param.9) | copy-start | bytes 12292
  0.7 18.0 %copy-start.3 = (s32[1024,1]{0,1:T(1,128)S(1)}, s32[1024,1]{0,1:T(1,128)}, u32[]{:S(2)}) copy-start(s32[1024,1]{0,1:T(1,128)} %param.8) | copy-start | bytes 12292

commit v5 on v4

--- a/solution.py
+++ b/solution.py
@@ -1,3 +1,5 @@
+import math
+
 import jax
 import jax.numpy as jnp
 from jax import lax
@@ -138,7 +140,10 @@
     padded = rows_ref.shape[0]
     owner = owner_ref[...]
     marks, rank = ranks_of(owner, shards)
-    position = owner * capacity + rank
+    side = math.isqrt(shards)
+    line = lax.div(owner, side)
+    place = lax.rem(lax.rem(owner, side) - line + side, side) * side + line
+    position = place * capacity + rank
     ids = row_ref[...]
     spot = iota((LANES, tokens), 0) - HALF
     id_rows = jnp.zeros((shards, LANES), jnp.float32)
@@ -169,12 +174,14 @@
     scale = jnp.maximum(jnp.max(jnp.abs(partial), axis=0, keepdims=True), 1e-30)
     steps = jnp.floor(partial * ((LEVELS - 1) / scale) + 0.5)
     steps = jnp.clip(steps, -(LEVELS - 1.0), LEVELS - 1.0)
-    fold = jnp.dot(
-        row_mask(width).astype(jnp.float32), jnp.where(fold_mask(width, 1), steps, 0.0),
-        precision=lax.Precision.HIGHEST, preferred_element_type=jnp.float32,
-    )
+    high = jnp.floor(steps * (1.0 / 128.0))
+    spots, lines = fold_mask(width, 1), row_mask(width).astype(jnp.float32).astype(jnp.bfloat16)
+    fold = jnp.zeros((8, LANES), jnp.float32)
+    for part, unit in ((high, 128.0), (steps - high * 128.0, 1.0)):
+        spread = jnp.where(spots, part, 0.0).astype(jnp.bfloat16)
+        fold = fold + unit * jnp.dot(lines, spread, preferred_element_type=jnp.float32)
     sub, lane = iota((8, LANES), 0), iota((8, LANES), 1)
-    extra = jnp.where((sub > 0) & (lane >= HALF), encode(jnp.floor(fold + 0.5)), 0.0)
+    extra = jnp.where((sub > 0) & (lane >= HALF), encode(fold), 0.0)
     for n in range(3):
         piece = scale.astype(jnp.bfloat16).astype(jnp.float32)
         extra = jnp.where((sub == 0) & (lane == SCALE_LANE + n), piece, extra)
@@ -189,7 +196,8 @@
             mine = got[n * capacity : (n + 1) * capacity]
             pieces += [mine[:, k : k + LANES] for k in range(0, padded - LANES, LANES)]
             last = mine[:, padded - LANES :]
-            shard = first + n
+            place = first + n
+            shard = place % side * side + (place % side + place // side) % side
             pieces.append(last[:8] + pltpu.roll(last[16:], HALF, 1))
             pieces.append(last[8:16] + jnp.where(sub == 0, extra + id_rows[shard : shard + 1], extra))
         size = out_ref.shape[0] // shards * PICK
@@ -311,7 +319,9 @@
     stats = lax.all_to_all(stats_call(e, dy, gain, sections), "section", 0, 0, tiled=True)
     message = rows_call(e, dy, gain, stats, owner, row, shards, capacity)
     message = message.reshape(shards, -1, LANES)
-    got = lax.all_to_all(message, "dp", 0, 0, tiled=True)
+    side = math.isqrt(shards)
+    order = [x * side + (x + k) % side for k in range(side) for x in range(side)]
+    got = lax.all_to_all(message, "dp", 0, 0, tiled=True, axis_index_groups=[order])
     table, gain_gradient = table_call(got.reshape(-1, LANES), shards, capacity, width, VOCAB // shards)
     return (table.T, gain_gradient.reshape(width))
 

time: 89.3 us -> 88 us (0.985)
  the two profiles are of different devices: /device:TPU:6 before, /device:TPU:2 now
where the time goes in v5:
time: 88 us; the launch traced here: 87.8 us
  blocking collectives  77.9 us (89%)
  Pallas kernels  9.24 us (10%)
    all_to_all x1, blocking collectives, on_device(): lax.all_to_all(message, 'dp', 0, 0, tiled=True, axis_index_groups=[order])  61.7 us
    all_to_all x1, blocking collectives, on_device(): lax.all_to_all(stats_call(e, dy, gain, sections), 'section', 0, 0, tiled=...  16.2 us
    pallas_call x1, Pallas kernels, table_call(): pl.pallas_call(lambda *refs: table_kernel(shards, capacity, *refs), grid=...  4.58 us
    pallas_call x1, Pallas kernels, rows_call(): pl.pallas_call(lambda *refs: rows_kernel(shards, capacity, *refs), in_spe...  2.85 us
    pallas_call x1, Pallas kernels, stats_call(): pl.pallas_call(stats_kernel, in_specs=[pl.BlockSpec(memory_space=pltpu.HB...  1.81 us

profile of v5, /device:TPU:2, one launch (start us, length us, event | category | flops | bytes accessed | tf_op | source)
XLA Modules:
  0.0 87.8 jit_solution(5892171362696164509)
XLA Ops:
  0.6 0.0 copy-start.2
  0.6 0.0 copy-start.1
  0.7 0.0 copy-start
  0.7 0.0 copy-start.4
  0.7 0.0 copy-start.3
  0.7 1.8 %shard_map.68 = f32[16,8,256]{2,1,0:T(8,128)S(1)} custom-call(bf16[448,1024]{1,0:T(8,128)(2,1)} %bitcast.11, bf16[448,1024]{1,0:T(8,128)(2,1)} %bitcast.13, f32[1,448]{1,0:T(1,128)} %bitcast.15), custom_call_target="tpu_custom_call" | custom-call | tf_op jit(solution)/shard_map/pallas_call | solution.py:265
  2.5 16.2 %all_to_all.10.refs_3_ = f32[16,8,256]{2,1,0:T(8,128)S(1)} all-to-all(f32[16,8,256]{2,1,0:T(8,128)S(1)} %shard_map.68), channel_id=1, replica_groups=mesh['section'=16,'dp'=64] {'section'}, dimensions={0} | all-to-all | bytes 262144 | tf_op jit(solution)/shard_map/all_to_all | solution.py:319
  18.7 0.0 copy-done.2
  18.7 0.0 copy-done.1
  18.7 0.0 copy-done
  18.7 0.0 copy-done.4
  18.7 0.0 copy-done.3
  18.7 2.9 %shard_map.69 = bf16[5632,128]{1,0:T(8,128)(2,1)S(1)} custom-call(bf16[448,1024]{1,0:T(8,128)(2,1)S(1)} %bitcast.12, bf16[448,1024]{1,0:T(8,128)(2,1)S(1)} %bitcast.14, f32[1,448]{1,0:T(1,128)S(1)} %bitcast.16, f32[16,8,256]{2,1,0:T(8,128)S(1)} %all_to_all.10.refs_3_, s32[1,1024]{1,0:T(1,128)S(1)} %bitcast.17, s32[1,1024]{1,0:T(1,128)S(1)} %bitcast.18), custom_call_target="tpu_custom_call" | custom-call | tf_op jit(solution)/shard_map/pallas_call | solution.py:284
  21.6 61.7 %all_to_all.11 = bf16[64,88,128]{2,1,0:T(8,128)(2,1)S(1)} all-to-all(bf16[64,88,128]{2,1,0:T(8,128)(2,1)S(1)} %bitcast.10), channel_id=1, replica_groups={{0,9,18,27,36,45,54,63,1,10,19,28,37,46,55,56,2,11,20,29,38,47,48,57,3,..., dimensions={0} | all-to-all | bytes 2883584 | tf_op jit(solution)/shard_map/all_to_all | solution.py:324
  83.3 4.6 %shard_map.70 = (bf16[448,2020]{1,0:T(8,128)(2,1)}, f32[1,448]{1,0:T(1,128)}) custom-call(bf16[5632,128]{1,0:T(8,128)(2,1)S(1)} %bitcast.9), custom_call_target="tpu_custom_call" | custom-call | tf_op jit(solution)/shard_map/pallas_call | solution.py:298
Async XLA Ops:
  0.6 18.0 %copy-start.2 = (f32[448]{0:T(512)S(1)}, f32[448]{0:T(512)}, u32[]{:S(2)}) copy-start(f32[448]{0:T(512)} %param.7) | copy-start | bytes 5380
  0.6 18.0 %copy-start.1 = (bf16[1024,448]{0,1:T(8,128)(2,1)S(1)}, bf16[1024,448]{0,1:T(8,128)(2,1)}, u32[]{:S(2)}) copy-start(bf16[1024,448]{0,1:T(8,128)(2,1)} %param.6) | copy-start | bytes 2752516
  0.7 18.0 %copy-start = (bf16[1024,448]{0,1:T(8,128)(2,1)S(1)}, bf16[1024,448]{0,1:T(8,128)(2,1)}, u32[]{:S(2)}) copy-start(bf16[1024,448]{0,1:T(8,128)(2,1)} %param.5) | copy-start | bytes 2752516
  0.7 18.0 %copy-start.4 = (s32[1024,1]{0,1:T(1,128)S(1)}, s32[1024,1]{0,1:T(1,128)}, u32[]{:S(2)}) copy-start(s32[1024,1]{0,1:T(1,128)} %param.9) | copy-start | bytes 12292
  0.7 18.0 %copy-start.3 = (s32[1024,1]{0,1:T(1,128)S(1)}, s32[1024,1]{0,1:T(1,128)}, u32[]{:S(2)}) copy-start(s32[1024,1]{0,1:T(1,128)} %param.8) | copy-start | bytes 12292

commit v6 on v5

--- a/solution.py
+++ b/solution.py
@@ -142,7 +142,7 @@
     marks, rank = ranks_of(owner, shards)
     side = math.isqrt(shards)
     line = lax.div(owner, side)
-    place = lax.rem(lax.rem(owner, side) - line + side, side) * side + line
+    place = lax.rem(line - lax.rem(owner, side) + side, side) * side + lax.rem(owner, side)
     position = place * capacity + rank
     ids = row_ref[...]
     spot = iota((LANES, tokens), 0) - HALF
@@ -197,7 +197,7 @@
             pieces += [mine[:, k : k + LANES] for k in range(0, padded - LANES, LANES)]
             last = mine[:, padded - LANES :]
             place = first + n
-            shard = place % side * side + (place % side + place // side) % side
+            shard = (place % side + place // side) % side * side + place % side
             pieces.append(last[:8] + pltpu.roll(last[16:], HALF, 1))
             pieces.append(last[8:16] + jnp.where(sub == 0, extra + id_rows[shard : shard + 1], extra))
         size = out_ref.shape[0] // shards * PICK
@@ -320,7 +320,7 @@
     message = rows_call(e, dy, gain, stats, owner, row, shards, capacity)
     message = message.reshape(shards, -1, LANES)
     side = math.isqrt(shards)
-    order = [x * side + (x + k) % side for k in range(side) for x in range(side)]
+    order = [(z + k) % side * side + z for k in range(side) for z in range(side)]
     got = lax.all_to_all(message, "dp", 0, 0, tiled=True, axis_index_groups=[order])
     table, gain_gradient = table_call(got.reshape(-1, LANES), shards, capacity, width, VOCAB // shards)
     return (table.T, gain_gradient.reshape(width))

time: 88 us -> 88.8 us (level)
  the two profiles are of different devices: /device:TPU:2 before, /device:TPU:1 now
where the time goes in v6:
time: 88.8 us; the launch traced here: 88.6 us
  blocking collectives  78.6 us (89%)
  Pallas kernels  9.24 us (10%)
    all_to_all x1, blocking collectives, on_device(): lax.all_to_all(message, 'dp', 0, 0, tiled=True, axis_index_groups=[order])  52.9 us
    all_to_all x1, blocking collectives, on_device(): lax.all_to_all(stats_call(e, dy, gain, sections), 'section', 0, 0, tiled=...  25.8 us
    pallas_call x1, Pallas kernels, table_call(): pl.pallas_call(lambda *refs: table_kernel(shards, capacity, *refs), grid=...  4.57 us
    pallas_call x1, Pallas kernels, rows_call(): pl.pallas_call(lambda *refs: rows_kernel(shards, capacity, *refs), in_spe...  2.85 us
    pallas_call x1, Pallas kernels, stats_call(): pl.pallas_call(stats_kernel, in_specs=[pl.BlockSpec(memory_space=pltpu.HB...  1.81 us

profile of v6, /device:TPU:1, one launch (start us, length us, event | category | flops | bytes accessed | tf_op | source)
XLA Modules:
  0.0 88.6 jit_solution(11018010631328893149)
XLA Ops:
  0.6 0.0 copy-start.2
  0.6 0.0 copy-start.1
  0.7 0.0 copy-start
  0.7 0.0 copy-start.4
  0.7 0.0 copy-start.3
  0.7 1.8 %shard_map.68 = f32[16,8,256]{2,1,0:T(8,128)S(1)} custom-call(bf16[448,1024]{1,0:T(8,128)(2,1)} %bitcast.11, bf16[448,1024]{1,0:T(8,128)(2,1)} %bitcast.13, f32[1,448]{1,0:T(1,128)} %bitcast.15), custom_call_target="tpu_custom_call" | custom-call | tf_op jit(solution)/shard_map/pallas_call | solution.py:265
  2.5 25.8 %all_to_all.10.refs_3_ = f32[16,8,256]{2,1,0:T(8,128)S(1)} all-to-all(f32[16,8,256]{2,1,0:T(8,128)S(1)} %shard_map.68), channel_id=1, replica_groups=mesh['section'=16,'dp'=64] {'section'}, dimensions={0} | all-to-all | bytes 262144 | tf_op jit(solution)/shard_map/all_to_all | solution.py:319
  28.3 0.0 copy-done.2
  28.3 0.0 copy-done.1
  28.3 0.0 copy-done
  28.3 0.0 copy-done.4
  28.3 0.0 copy-done.3
  28.3 2.9 %shard_map.69 = bf16[5632,128]{1,0:T(8,128)(2,1)S(1)} custom-call(bf16[448,1024]{1,0:T(8,128)(2,1)S(1)} %bitcast.12, bf16[448,1024]{1,0:T(8,128)(2,1)S(1)} %bitcast.14, f32[1,448]{1,0:T(1,128)S(1)} %bitcast.16, f32[16,8,256]{2,1,0:T(8,128)S(1)} %all_to_all.10.refs_3_, s32[1,1024]{1,0:T(1,128)S(1)} %bitcast.17, s32[1,1024]{1,0:T(1,128)S(1)} %bitcast.18), custom_call_target="tpu_custom_call" | custom-call | tf_op jit(solution)/shard_map/pallas_call | solution.py:284
  31.2 52.9 %all_to_all.11 = bf16[64,88,128]{2,1,0:T(8,128)(2,1)S(1)} all-to-all(bf16[64,88,128]{2,1,0:T(8,128)(2,1)S(1)} %bitcast.10), channel_id=1, replica_groups={{0,9,18,27,36,45,54,63,8,17,26,35,44,53,62,7,16,25,34,43,52,61,6,15,24,..., dimensions={0} | all-to-all | bytes 2883584 | tf_op jit(solution)/shard_map/all_to_all | solution.py:324
  84.0 4.6 %shard_map.70 = (bf16[448,2020]{1,0:T(8,128)(2,1)}, f32[1,448]{1,0:T(1,128)}) custom-call(bf16[5632,128]{1,0:T(8,128)(2,1)S(1)} %bitcast.9), custom_call_target="tpu_custom_call" | custom-call | tf_op jit(solution)/shard_map/pallas_call | solution.py:298
Async XLA Ops:
  0.6 27.6 %copy-start.2 = (f32[448]{0:T(512)S(1)}, f32[448]{0:T(512)}, u32[]{:S(2)}) copy-start(f32[448]{0:T(512)} %param.7) | copy-start | bytes 5380
  0.6 27.6 %copy-start.1 = (bf16[1024,448]{0,1:T(8,128)(2,1)S(1)}, bf16[1024,448]{0,1:T(8,128)(2,1)}, u32[]{:S(2)}) copy-start(bf16[1024,448]{0,1:T(8,128)(2,1)} %param.6) | copy-start | bytes 2752516
  0.7 27.6 %copy-start = (bf16[1024,448]{0,1:T(8,128)(2,1)S(1)}, bf16[1024,448]{0,1:T(8,128)(2,1)}, u32[]{:S(2)}) copy-start(bf16[1024,448]{0,1:T(8,128)(2,1)} %param.5) | copy-start | bytes 2752516
  0.7 27.6 %copy-start.4 = (s32[1024,1]{0,1:T(1,128)S(1)}, s32[1024,1]{0,1:T(1,128)}, u32[]{:S(2)}) copy-start(s32[1024,1]{0,1:T(1,128)} %param.9) | copy-start | bytes 12292
  0.7 27.6 %copy-start.3 = (s32[1024,1]{0,1:T(1,128)S(1)}, s32[1024,1]{0,1:T(1,128)}, u32[]{:S(2)}) copy-start(s32[1024,1]{0,1:T(1,128)} %param.8) | copy-start | bytes 12292
